TPU v7x, 128 devices: a whole 4x4x4 slice. The times are simulated.
128 devices in a mesh: row: 16 (over y, x_hi, core), rep: 8 (over x_lo, z).
Axes of the slice: x: 4 (x_hi: 2, x_lo: 2; x = x_hi * 2 + x_lo), y: 4, z: 4, core: 2. Of those that a mesh axis runs over, the one named last changes fastest.
Arguments:
- features: float32 [32768, 256], P('row'), may hold values from -6 to 6
- adjacency_tiles: float32 [16, 8, 256, 128, 128], P('row', 'rep'), may hold values from -0.25 to 0.25
- tile_rows: int32 [16, 8, 256], P('row', 'rep'), may hold values from 0 to 15, as said below
- tile_cols: int32 [16, 8, 256], P('row', 'rep'), may hold values from 0 to 31, as said below
- tile_counts: int32 [16, 8], P('row', 'rep'), may hold values from 32 to 256, as said below
- plan: int32 [8, 2], replicated, may hold values from 0 to 15, as said below
- weights: float32 [2, 256, 256], replicated, may hold values from -0.375 to 0.375
Outputs:
- embedded: float32 [32768, 256], P(('row', 'rep'))
Inputs may be any that keep to these rules, and one draw needn't show every extreme that they name: Within one block row and replica the listed positions (tile_rows, tile_cols) are distinct. Within one block row and replica the listed positions (tile_rows, tile_cols) are distinct. `tile_counts`: some block row and replica lists exactly 256 tiles. `plan`: every block row 0 to 15 appears exactly once in the table.
All inputs are finite; a program needn't handle non-finite values.
Results may differ from a plain program's by a relative error of at most 0.0003.
Values sent between devices are 32-bit elements; how exact they have to be, the bound alone decides.
A program may use at most 128 MiB of HBM per device.

v0:
```python
import math

import jax
import jax.numpy as jnp
from jax import lax
from jax.sharding import PartitionSpec as P


def from_root(value, axis, source):
    kept = jnp.where(lax.axis_index(axis) == source, value, 0).astype(value.dtype)
    return lax.psum(kept, axis)


def tile_sum(received, tiles_here, rows_here, cols_here, count_here, row_tiles):
    tile_slots = tiles_here.shape[0]
    tile_edge = received.shape[1]
    feat_width = received.shape[2]
    group_size = math.gcd(tile_slots, 64)
    steps_total = tile_slots // group_size
    slot_ids = jnp.arange(tile_slots, dtype=jnp.int32)
    live_mask = (slot_ids < count_here).astype(jnp.float32)
    lane_ids = jnp.arange(row_tiles, dtype=jnp.int32)

    def advance(running, packet):
        block_tiles, block_rows, block_cols, block_live = packet
        sources = jnp.take(received, block_cols, axis=0)
        product = jnp.einsum("tij,tjf->tif", block_tiles, sources, precision=lax.Precision.HIGHEST)
        product = product * block_live[:, None, None]
        placing = (block_rows[None, :] == lane_ids[:, None]).astype(jnp.float32)
        added = jnp.dot(
            placing,
            product.reshape(group_size, tile_edge * feat_width),
            precision=lax.Precision.HIGHEST,
        )
        return (running + added, None)

    packets = (
        tiles_here.reshape(steps_total, group_size, tile_edge, tile_edge),
        rows_here.reshape(steps_total, group_size),
        cols_here.reshape(steps_total, group_size),
        live_mask.reshape(steps_total, group_size),
    )
    start = jnp.zeros((row_tiles, tile_edge * feat_width), jnp.float32)
    running, unused = lax.scan(advance, start, packets)
    return running.reshape(row_tiles * tile_edge, feat_width)


def shards(features, adjacency_tiles, tile_rows, tile_cols, tile_counts, plan, weights):
    replica = lax.axis_index("rep")
    block_len = features.shape[0]
    feat_width = features.shape[1]
    tile_edge = adjacency_tiles.shape[-1]
    row_tiles = block_len // tile_edge
    section_total = plan.shape[1]
    layer_total = weights.shape[0]
    share_rows = block_len // lax.axis_size("rep")
    section_roots = lax.dynamic_index_in_dim(plan, replica, 0, keepdims=False)
    tiles_here = adjacency_tiles[0, 0]
    rows_here = tile_rows[0, 0]
    cols_here = tile_cols[0, 0]
    count_here = tile_counts[0, 0]
    current = features
    result = features
    for layer_num in range(layer_total):
        received = jnp.zeros((section_total * block_len, feat_width), jnp.float32)
        for section_num in range(section_total):
            root_now = lax.dynamic_index_in_dim(section_roots, section_num, 0, keepdims=False)
            arrived = from_root(current, "row", root_now)
            received = lax.dynamic_update_slice_in_dim(
                received, arrived, section_num * block_len, 0
            )
        received = received.reshape(section_total * row_tiles, tile_edge, feat_width)
        partial_value = tile_sum(received, tiles_here, rows_here, cols_here, count_here, row_tiles)
        summed = lax.psum(partial_value, "rep")
        current = jnp.maximum(
            jnp.dot(summed, weights[layer_num], precision=lax.Precision.HIGHEST), 0.0
        )
        result = lax.dynamic_slice_in_dim(current, replica * share_rows, share_rows, 0)
    return result


def solution(mesh):
    return jax.shard_map(
        shards,
        mesh=mesh,
        in_specs=(
            P("row", None),
            P("row", "rep", None, None, None),
            P("row", "rep", None),
            P("row", "rep", None),
            P("row", "rep"),
            P(),
            P(),
        ),
        out_specs=P(("row", "rep"), None),
        check_vma=False,
    )
```

profile of v0, /device:TPU:0, one launch (start us, length us, event | category | flops | bytes accessed | tf_op | source)
XLA Modules:
  0.0 774.9 jit_solution(13985871500176269635)
XLA Ops:
  15.8 157.1 %all-reduce.13.cloned.1.call-done = (f32[2048,256]{1,0:T(8,128)}, f32[2048,256]{1,0:T(8,128)}) async-done(((f32[2048,256]{1,0:T(8,128)}, f32[2048,256]{1,0:T(8,128)}), (f32[2048,256]{1,0:T(8,128)}, f32[2048,256]{1,0:T(8,128)})) %all-reduce.13.cloned.1.call-update) | async-done | bytes 4194320 | tf_op jit(solution)/shard_map/psum | solution.py:11
  177.3 126.4 %while.22 = (s32[]{:T(128)}, f32[16,32768]{1,0:T(8,128)S(1)}, s32[4,64]{1,0:T(4,128)S(1)}, f32[4,64,128,128]{3,2,1,0:T(8,128)}, s32[4,64]{1,0:T(4,128)S(1)}, /*i...) while((s32[]{:T(128)}, f32[16,32768]{1,0:T(8,128)S(1)}, ...), condition=%wide.region_3.5_spmd.clone, body=%wide.region_2.4_spmd.clone.sunk | while | flops 3629124096 | bytes 67116272 | solution.py:44
  177.3 6.5 gather_fusion
  183.8 11.7 %broadcast_multiply_fusion.4 = f32[64,128,256]{2,1,0:T(8,128)S(1)} fusion(f32[64]{0:T(128)S(1)} %fusion.60, f32[64,128,256]{2,1,0:T(8,128)} %gather_fusion, pred[64]{0:T(512)(128)(4,1)S(1)} %get-tuple-element.270, f32[4,64,128,128]{3,2,1,0:T(8,128)} %get-tuple-element.301, s32[]{:T(128)} %get-tuple-element.289), kind=kOutput, calls=%fused_computation.9.clone.1 | convolution fusion | flops 3225419776 | bytes 20972352 | tf_op jit(solution)/shard_map/while/body/eval_jaxpr/tij,tjf->tif/dot_general | solution.py:27
  195.6 8.0 %copy.12 = f32[8,8,128,256]{3,1,2,0:T(8,128)} copy(f32[8,8,128,256]{3,2,1,0:T(8,128)S(1)} %bitcast.77) | data formatting | bytes 16777216 | tf_op jit(solution)/shard_map/while
  208.9 6.5 gather_fusion
  215.4 11.7 %broadcast_multiply_fusion.4 = f32[64,128,256]{2,1,0:T(8,128)S(1)} fusion(f32[64]{0:T(128)S(1)} %fusion.60, f32[64,128,256]{2,1,0:T(8,128)} %gather_fusion, pred[64]{0:T(512)(128)(4,1)S(1)} %get-tuple-element.270, f32[4,64,128,128]{3,2,1,0:T(8,128)} %get-tuple-element.301, s32[]{:T(128)} %get-tuple-element.289), kind=kOutput, calls=%fused_computation.9.clone.1 | convolution fusion | flops 3225419776 | bytes 20972352 | tf_op jit(solution)/shard_map/while/body/eval_jaxpr/tij,tjf->tif/dot_general | solution.py:27
  227.2 8.0 %copy.12 = f32[8,8,128,256]{3,1,2,0:T(8,128)} copy(f32[8,8,128,256]{3,2,1,0:T(8,128)S(1)} %bitcast.77) | data formatting | bytes 16777216 | tf_op jit(solution)/shard_map/while
  240.5 6.5 gather_fusion
  247.0 11.7 %broadcast_multiply_fusion.4 = f32[64,128,256]{2,1,0:T(8,128)S(1)} fusion(f32[64]{0:T(128)S(1)} %fusion.60, f32[64,128,256]{2,1,0:T(8,128)} %gather_fusion, pred[64]{0:T(512)(128)(4,1)S(1)} %get-tuple-element.270, f32[4,64,128,128]{3,2,1,0:T(8,128)} %get-tuple-element.301, s32[]{:T(128)} %get-tuple-element.289), kind=kOutput, calls=%fused_computation.9.clone.1 | convolution fusion | flops 3225419776 | bytes 20972352 | tf_op jit(solution)/shard_map/while/body/eval_jaxpr/tij,tjf->tif/dot_general | solution.py:27
  258.8 8.0 %copy.12 = f32[8,8,128,256]{3,1,2,0:T(8,128)} copy(f32[8,8,128,256]{3,2,1,0:T(8,128)S(1)} %bitcast.77) | data formatting | bytes 16777216 | tf_op jit(solution)/shard_map/while
  272.1 6.5 gather_fusion
  278.6 11.7 %broadcast_multiply_fusion.4 = f32[64,128,256]{2,1,0:T(8,128)S(1)} fusion(f32[64]{0:T(128)S(1)} %fusion.60, f32[64,128,256]{2,1,0:T(8,128)} %gather_fusion, pred[64]{0:T(512)(128)(4,1)S(1)} %get-tuple-element.270, f32[4,64,128,128]{3,2,1,0:T(8,128)} %get-tuple-element.301, s32[]{:T(128)} %get-tuple-element.289), kind=kOutput, calls=%fused_computation.9.clone.1 | convolution fusion | flops 3225419776 | bytes 20972352 | tf_op jit(solution)/shard_map/while/body/eval_jaxpr/tij,tjf->tif/dot_general | solution.py:27
  290.4 8.0 %copy.12 = f32[8,8,128,256]{3,1,2,0:T(8,128)} copy(f32[8,8,128,256]{3,2,1,0:T(8,128)S(1)} %bitcast.77) | data formatting | bytes 16777216 | tf_op jit(solution)/shard_map/while
  298.4 5.3 convolution_add_fusion.4
  305.5 81.5 %all-reduce.7.cloned.1.call-done = f32[2048,256]{1,0:T(8,128)} async-done(((f32[2048,256]{1,0:T(8,128)}), f32[2048,256]{1,0:T(8,128)}) %all-reduce.7.cloned.1.call-update) | async-done | bytes 2097168 | tf_op jit(solution)/shard_map/psum | solution.py:74
  386.9 5.4 broadcast_select_fusion.1
  392.4 157.8 %all-reduce.11.cloned.1.call-done = (f32[2048,256]{1,0:T(8,128)}, f32[2048,256]{1,0:T(8,128)}) async-done(((f32[2048,256]{1,0:T(8,128)}, f32[2048,256]{1,0:T(8,128)}), (f32[2048,256]{1,0:T(8,128)}, f32[2048,256]{1,0:T(8,128)})) %all-reduce.11.cloned.1.call-update) | async-done | bytes 4194320 | tf_op jit(solution)/shard_map/psum | solution.py:11
  554.7 126.4 %while.23 = (s32[]{:T(128)}, f32[16,32768]{1,0:T(8,128)S(1)}, s32[4,64]{1,0:T(4,128)S(1)}, f32[4,64,128,128]{3,2,1,0:T(8,128)}, s32[4,64]{1,0:T(4,128)S(1)}, /*i...) while((s32[]{:T(128)}, f32[16,32768]{1,0:T(8,128)S(1)}, ...), condition=%wide.region_8.10_spmd.clone, body=%wide.region_7.9_spmd.clone.sunk | while | flops 3629124096 | bytes 67116272 | solution.py:44
  554.7 6.5 gather_fusion.1
  561.2 11.7 %broadcast_multiply_fusion.5 = f32[64,128,256]{2,1,0:T(8,128)S(1)} fusion(f32[64]{0:T(128)S(1)} %fusion.65, f32[64,128,256]{2,1,0:T(8,128)} %gather_fusion.1, pred[64]{0:T(512)(128)(4,1)S(1)} %get-tuple-element.279, f32[4,64,128,128]{3,2,1,0:T(8,128)} %get-tuple-element.328, s32[]{:T(128)} %get-tuple-element.316), kind=kOutput, calls=%fused_computation.30.clone.1 | convolution fusion | flops 3225419776 | bytes 20972352 | tf_op jit(solution)/shard_map/while/body/eval_jaxpr/tij,tjf->tif/dot_general | solution.py:27
  572.9 8.0 %copy.13 = f32[8,8,128,256]{3,1,2,0:T(8,128)} copy(f32[8,8,128,256]{3,2,1,0:T(8,128)S(1)} %bitcast.78) | data formatting | bytes 16777216 | tf_op jit(solution)/shard_map/while
  586.3 6.5 gather_fusion.1
  592.8 11.7 %broadcast_multiply_fusion.5 = f32[64,128,256]{2,1,0:T(8,128)S(1)} fusion(f32[64]{0:T(128)S(1)} %fusion.65, f32[64,128,256]{2,1,0:T(8,128)} %gather_fusion.1, pred[64]{0:T(512)(128)(4,1)S(1)} %get-tuple-element.279, f32[4,64,128,128]{3,2,1,0:T(8,128)} %get-tuple-element.328, s32[]{:T(128)} %get-tuple-element.316), kind=kOutput, calls=%fused_computation.30.clone.1 | convolution fusion | flops 3225419776 | bytes 20972352 | tf_op jit(solution)/shard_map/while/body/eval_jaxpr/tij,tjf->tif/dot_general | solution.py:27
  604.5 8.0 %copy.13 = f32[8,8,128,256]{3,1,2,0:T(8,128)} copy(f32[8,8,128,256]{3,2,1,0:T(8,128)S(1)} %bitcast.78) | data formatting | bytes 16777216 | tf_op jit(solution)/shard_map/while
  617.9 6.5 gather_fusion.1
  624.4 11.7 %broadcast_multiply_fusion.5 = f32[64,128,256]{2,1,0:T(8,128)S(1)} fusion(f32[64]{0:T(128)S(1)} %fusion.65, f32[64,128,256]{2,1,0:T(8,128)} %gather_fusion.1, pred[64]{0:T(512)(128)(4,1)S(1)} %get-tuple-element.279, f32[4,64,128,128]{3,2,1,0:T(8,128)} %get-tuple-element.328, s32[]{:T(128)} %get-tuple-element.316), kind=kOutput, calls=%fused_computation.30.clone.1 | convolution fusion | flops 3225419776 | bytes 20972352 | tf_op jit(solution)/shard_map/while/body/eval_jaxpr/tij,tjf->tif/dot_general | solution.py:27
  636.1 8.0 %copy.13 = f32[8,8,128,256]{3,1,2,0:T(8,128)} copy(f32[8,8,128,256]{3,2,1,0:T(8,128)S(1)} %bitcast.78) | data formatting | bytes 16777216 | tf_op jit(solution)/shard_map/while
  649.5 6.5 gather_fusion.1
  656.0 11.7 %broadcast_multiply_fusion.5 = f32[64,128,256]{2,1,0:T(8,128)S(1)} fusion(f32[64]{0:T(128)S(1)} %fusion.65, f32[64,128,256]{2,1,0:T(8,128)} %gather_fusion.1, pred[64]{0:T(512)(128)(4,1)S(1)} %get-tuple-element.279, f32[4,64,128,128]{3,2,1,0:T(8,128)} %get-tuple-element.328, s32[]{:T(128)} %get-tuple-element.316), kind=kOutput, calls=%fused_computation.30.clone.1 | convolution fusion | flops 3225419776 | bytes 20972352 | tf_op jit(solution)/shard_map/while/body/eval_jaxpr/tij,tjf->tif/dot_general | solution.py:27
  667.7 8.0 %copy.13 = f32[8,8,128,256]{3,1,2,0:T(8,128)} copy(f32[8,8,128,256]{3,2,1,0:T(8,128)S(1)} %bitcast.78) | data formatting | bytes 16777216 | tf_op jit(solution)/shard_map/while
  682.6 81.7 %all-reduce.9.cloned.1.call-done = f32[2048,256]{1,0:T(8,128)} async-done(((f32[2048,256]{1,0:T(8,128)}), f32[2048,256]{1,0:T(8,128)}) %all-reduce.9.cloned.1.call-update) | async-done | bytes 2097168 | tf_op jit(solution)/shard_map/psum | solution.py:74
  (74 shorter events, 61.2 us)
Async XLA Ops:
  6.5 0.7 copy-start
  6.5 166.3 %all-reduce.13.cloned.1.call-start = ((), (), s32[]{:S(2)}) async-start(), calls=%async_computation.3 | async-start | bytes 8388608 | tf_op jit(solution)/shard_map/psum | solution.py:11
  13.0 0.7 copy-start.3
  13.0 1.4 copy-start.4
  13.0 373.9 %all-reduce.7.cloned.1.call-start = ((), (), s32[]{:S(2)}) async-start(), calls=%async_computation | async-start | bytes 4194304 | tf_op jit(solution)/shard_map/psum | solution.py:74
  305.2 81.7 %copy-start.2 = (f32[2,256,256]{2,1,0:T(8,128)S(1)}, f32[2,256,256]{2,1,0:T(8,128)}, u32[]{:S(2)}) copy-start(f32[2,256,256]{2,1,0:T(8,128)} %param.19) | copy-start | bytes 1572868
  305.2 245.0 %all-reduce.11.cloned.1.call-start = ((), (), s32[]{:S(2)}) async-start(), calls=%async_computation.2 | async-start | bytes 8388608 | tf_op jit(solution)/shard_map/psum | solution.py:11
  392.3 371.9 %all-reduce.9.cloned.1.call-start = ((), (), s32[]{:S(2)}) async-start(), calls=%async_computation.1 | async-start | bytes 4194304 | tf_op jit(solution)/shard_map/psum | solution.py:74
  682.6 85.8 %copy-start.1 = (s32[8,2]{0,1:T(2,128)S(1)}, s32[8,2]{0,1:T(2,128)}, u32[]{:S(2)}) copy-start(s32[8,2]{0,1:T(2,128)} %param.18) | copy-start | bytes 196
Sparse Core Ops, SparseCore 0:
  13.1 159.6 all-reduce.12
  305.4 81.5 all-reduce.6
  392.4 157.7 all-reduce.10
  682.7 81.5 all-reduce.8
where the time goes:
time: 776 us; the launch traced here: 775 us
  waiting for transfers between devices  478 us (62%)
  matrix products  145 us (19%)
  local copies, waits for them, and re-layouts  121 us (16%)
  between operations  15.1 us (2%)
  other arithmetic  14.9 us (2%)
    psum x2, waiting for transfers between devices, from_root(): return lax.psum(kept, axis)  315 us
    psum x2, waiting for transfers between devices, shards(): summed = lax.psum(partial_value, 'rep')  163 us
    dot_general x8, matrix products, advance(): jnp.einsum('tij,tjf->tif', block_tiles, sources, precision=lax.Precision....  93.9 us
    while x8, local copies, waits for them, and re-layouts  63.6 us
    gather x8, local copies, waits for them, and re-layouts, advance(): sources = jnp.take(received, block_cols, axis=0)  52 us
    dot_general x8, matrix products, advance(): jnp.dot(placing, product.reshape(group_size, tile_edge * feat_width), pre...  42.7 us
  transfers between devices with their start and end apart: 4, of which 4 were waited for; matrix products, arithmetic and copies ran while one was open for 0% of the time, Pallas kernels for 0%

commit v1 on v0

v1 whole, which is shorter than its diff:
```python
import functools

import jax
import jax.numpy as jnp
from jax import lax
from jax.experimental import pallas as pl
from jax.experimental.pallas import tpu as pltpu
from jax.sharding import PartitionSpec as P

BF = jnp.bfloat16
F32 = jnp.float32
MESH = pl.DeviceIdType.MESH
Y, XH, C, XL, Z = 4, 2, 2, 2, 4
GROUP = 16
STAGES = 4
COPIES = 160


def mm(a, b):
    return jnp.dot(a, b, preferred_element_type=F32)


def split(v):
    high = v.astype(BF)
    return high, (v - high.astype(F32)).astype(BF)


def kernel(
    pos, plan, x_ref, tiles, w_ref, o_ref,
    stage, hi, lo, land, acc, acc_out, buf_00, buf_01, buf_10, buf_11, send_b, hid, bh, bl,
    r1, r2, q1, q3, r3, f1, f2, g1, g3, f3,
    stage_sem, ssem, rsem, a_send, a_recv, b_send, b_recv,
):
    row, rep = lax.axis_index("row"), lax.axis_index("rep")
    y, xh, c = row // 4, (row // 2) % 2, row % 2
    xl, z = rep // 4, rep % 4

    def rows_dev(dy, dx, dc):
        return ((y + dy) % 4) * 4 + ((xh + dx) % 2) * 2 + (c + dc) % 2

    def reps_dev(dx, dz):
        return ((xl + dx) % 2) * 4 + (z + dz) % 4

    row_peers = [
        rows_dev(a, b, d) for a in range(4) for b in range(2) for d in range(2) if (a, b, d) != (0, 0, 0)
    ]
    rep_peers = [reps_dev(a, b) for a in range(2) for b in range(4) if (a, b) != (0, 0)]

    def load_tiles(g, slot):
        return pltpu.make_async_copy(
            tiles.at[pl.ds(g * GROUP, GROUP)], stage.at[slot], stage_sem.at[slot]
        )

    for g in range(STAGES):
        load_tiles(g, g).start()

    barrier = pltpu.get_barrier_semaphore()
    for peer in row_peers:
        pl.semaphore_signal(barrier, inc=1, device_id=(peer, rep), device_id_type=MESH)
    for peer in rep_peers:
        pl.semaphore_signal(barrier, inc=1, device_id=(row, peer), device_id_type=MESH)
    pl.semaphore_wait(barrier, 22)

    used = [0]
    sent = []

    def remote(src, dst, dev):
        n = used[0]
        used[0] += 1
        copy = pltpu.make_async_remote_copy(
            src_ref=src, dst_ref=dst, send_sem=ssem.at[n], recv_sem=rsem.at[n],
            device_id=dev, device_id_type=MESH,
        )
        sent.append(copy)
        copy.start()
        return copy

    buf_a = ((buf_00, buf_01), (buf_10, buf_11))

    def send_a(layer, h, source):
        for peer in row_peers:
            pltpu.make_async_remote_copy(
                src_ref=source(peer), dst_ref=buf_a[layer][h].at[row],
                send_sem=a_send.at[layer, h], recv_sem=a_recv.at[layer, h],
                device_id=(peer, rep), device_id_type=MESH,
            ).start()
        pltpu.make_async_copy(source(row), buf_a[layer][h].at[row], a_recv.at[layer, h]).start()

    def turn(layer, h):
        whole = buf_a[layer][h]
        pltpu.make_async_copy(whole, whole, a_recv.at[layer, h]).wait()
        for k in range(8):
            for s in range(2):
                send_b[layer, h, k, s] = buf_a[layer][h][plan[k * 2 + s]]
        for peer in rep_peers:
            pltpu.make_async_remote_copy(
                src_ref=send_b.at[layer, h, peer], dst_ref=land.at[layer, :, h, row, rep],
                send_sem=b_send.at[layer, h], recv_sem=b_recv.at[layer, h],
                device_id=(row, peer), device_id_type=MESH,
            ).start()
        pltpu.make_async_copy(
            send_b.at[layer, h, rep], land.at[layer, :, h, row, rep], b_recv.at[layer, h]
        ).start()

    def wait_b(layer, h):
        mine = land.at[layer, :, h, row]
        pltpu.make_async_copy(mine, mine, b_recv.at[layer, h]).wait()

    def convert(first, last):
        def one(g, carry):
            slot = lax.rem(g, STAGES)
            load_tiles(g, slot).wait()

            def tile(t, inner):
                high, low = split(stage[slot, t])
                hi[g * GROUP + t] = high
                lo[g * GROUP + t] = low
                return inner

            lax.fori_loop(0, GROUP, tile, 0, unroll=4)

            @pl.when(g + STAGES < 256 // GROUP)
            def _():
                load_tiles(g + STAGES, slot).start()

            return carry

        lax.fori_loop(first, last, one, 0)

    def products(layer, h, yy, out, row_tiles, whole=True):
        def one(j, carry):
            q = yy * 2 + j
            t = h * 8 + q
            f0 = land[layer, 0, h, pl.ds(q * 2, 2)].reshape(128, 256)
            f1_ = land[layer, 1, h, pl.ds(q * 2, 2)].reshape(128, 256)
            bh[0:128], bl[0:128] = split(f0)
            bh[128:256], bl[128:256] = split(f1_)
            for i in row_tiles:
                a0, a1 = pos[i * 32 + t], pos[i * 32 + 16 + t]
                top = jnp.concatenate([hi[a0], hi[a1]], axis=1)
                low = jnp.concatenate([lo[a0], lo[a1]], axis=1)
                added = mm(top, bh[...]) + mm(top, bl[...]) + mm(low, bh[...])
                out[2 * i : 2 * i + 2] += added.reshape(2, 8, 8, 256)
            return carry

        lax.fori_loop(0, 2, one, 0)

    class Gather:
        def __init__(self, layer, h):
            self.l, self.h = layer, h

        def piece(self, yy, xx, cc):
            return land.at[self.l, :, self.h, (yy % 4) * 4 + (xx % 2) * 2 + cc]

        def half(self, s, yy, xx, cc):
            return land.at[self.l, s, self.h, (yy % 4) * 4 + (xx % 2) * 2 + cc]

        def move(self, ref, dy, dx, dc):
            return remote(ref, ref, (rows_dev(dy, dx, dc), rep))

        def own(self):
            mine = self.piece(y, xh, c)
            self.x = self.move(mine, 0, 1, 0)
            self.up = [self.move(mine, 1, 0, 0), None]
            self.down = [self.move(mine, 3, 0, 0), None]
            self.core = {"y": [self.move(mine, 0, 0, 1)]}

        def partner(self):
            self.x.wait_recv()
            got = self.piece(y, xh + 1, c)
            self.up[1] = self.move(got, 1, 0, 0)
            self.down[1] = self.move(got, 3, 0, 0)
            self.core["y"].append(self.move(got, 0, 0, 1))

        def pass_on(self, n):
            self.up[n].wait_recv()
            up2 = self.move(self.half(0, y + 3, xh + n, c), 1, 0, 0)
            to_core = self.move(self.piece(y + 3, xh + n, c), 0, 0, 1)
            self.core.setdefault("m", []).append(to_core)
            self.down[n].wait_recv()
            down2 = self.move(self.half(1, y + 1, xh + n, c), 3, 0, 0)
            to_core = self.move(self.piece(y + 1, xh + n, c), 0, 0, 1)
            self.core.setdefault("p", []).append(to_core)
            self.core.setdefault("far", []).append((up2, down2))

        def far(self, n):
            up2, down2 = self.core["far"][n]
            up2.wait_recv()
            a = self.move(self.half(0, y + 2, xh + n, c), 0, 0, 1)
            down2.wait_recv()
            b = self.move(self.half(1, y + 2, xh + n, c), 0, 0, 1)
            self.core.setdefault("f", []).extend([a, b])

        def ready(self, name):
            for copy in self.core[name]:
                copy.wait_recv()

    def gather_and_multiply(layer, out, first_rows, rest_rows, begin_sum):
        every = range(16)
        a, b = Gather(layer, 0), Gather(layer, 1)
        wait_b(layer, 0)
        a.own()
        yield
        wait_b(layer, 1)
        b.own()
        a.partner()
        a.pass_on(0)
        b.partner()
        a.ready("y")
        products(layer, 0, y, out, every)
        a.pass_on(1)
        b.pass_on(0)
        a.ready("m")
        products(layer, 0, (y + 3) % 4, out, every)
        a.far(0)
        b.pass_on(1)
        a.ready("p")
        products(layer, 0, (y + 1) % 4, out, every)
        a.far(1)
        b.far(0)
        a.ready("f")
        products(layer, 0, (y + 2) % 4, out, every)
        b.far(1)
        b.ready("y")
        products(layer, 1, y, out, every)
        b.ready("m")
        products(layer, 1, (y + 3) % 4, out, every)
        b.ready("p")
        b.ready("f")
        products(layer, 1, (y + 1) % 4, out, first_rows)
        products(layer, 1, (y + 2) % 4, out, first_rows)
        begin_sum()
        products(layer, 1, (y + 1) % 4, out, rest_rows)
        products(layer, 1, (y + 2) % 4, out, rest_rows)

    class Reduce:
        def __init__(self, h, part, r1, r2, q1, q3, r3):
            self.h, self.part = h, part
            self.r1, self.r2, self.q1, self.q3, self.r3 = (
                r1.at[h], r2.at[h], q1.at[h], q3.at[h], r3.at[h]
            )

        def start(self):
            up, down = (row, reps_dev(0, 1)), (row, reps_dev(0, 3))
            self.raw = [
                remote(self.part(reps_dev(0, 2) % 4), self.r1.at[0], up),
                remote(self.part(4 + reps_dev(0, 2) % 4), self.r1.at[1], down),
            ]
            zu, zd = (z + 1) % 4, (z + 3) % 4
            self.second = [
                remote(self.part(4 + zu), self.r2.at[0, 1], up),
                remote(self.part(zd), self.r2.at[1, 0], down),
            ]

        def pass_on(self):
            up, down = (row, reps_dev(0, 1)), (row, reps_dev(0, 3))
            zu, zd = (z + 1) % 4, (z + 3) % 4
            self.raw[0].wait_recv()
            self.q1[0] = self.part(zu)[...] + self.r1[0]
            self.second.append(remote(self.q1.at[0], self.r2.at[0, 0], up))
            self.raw[1].wait_recv()
            self.q1[1] = self.part(4 + zd)[...] + self.r1[1]
            self.second.append(remote(self.q1.at[1], self.r2.at[1, 1], down))

        def cross(self):
            for copy in self.second:
                copy.wait_recv()
            other = 1 - xl
            self.q3[...] = self.part(other * 4 + z)[...] + self.r2[0, other] + self.r2[1, other]
            self.last = remote(self.q3, self.r3, (row, reps_dev(1, 0)))

        def finish(self, layer):
            mine = self.part(rep)[...] + self.r2[0, xl] + self.r2[1, xl]
            self.last.wait_recv()
            total = (mine + self.r3[...]).reshape(128, 256)
            wh, wl = split(w_ref[layer])
            th, tl = split(total)
            return jnp.maximum(mm(th, wh) + mm(th, wl) + mm(tl, wh), 0.0)

    for h in range(2):
        send_a(0, h, lambda p: x_ref.at[h, p, rep])
    hi[256] = jnp.zeros((128, 128), BF)
    lo[256] = jnp.zeros((128, 128), BF)

    def clear(i, carry):
        acc[i] = jnp.zeros((8, 8, 256), F32)
        acc_out[i] = jnp.zeros((8, 8, 256), F32)
        return carry

    lax.fori_loop(0, 32, clear, 0)
    convert(0, 6)
    turn(0, 0)
    turn(0, 1)
    convert(6, 256 // GROUP)

    mid = [
        Reduce(h, lambda k, h=h: acc.at[pl.ds(16 * h, 16), k], r1, r2, q1, q3, r3) for h in range(2)
    ]
    for _ in gather_and_multiply(0, acc, range(8), range(8, 16), mid[0].start):
        pass
    mid[1].start()
    mid[0].pass_on()
    mid[0].cross()
    mid[1].pass_on()
    hid[0] = mid[0].finish(0).reshape(16, 8, 256)
    send_a(1, 0, lambda p: hid.at[0, p])
    turn(1, 0)
    mid[1].cross()
    step = gather_and_multiply(
        1, acc_out, range(0, 16, 2), range(1, 16, 2), lambda: end[0].start()
    )
    end = [
        Reduce(h, lambda k, h=h: acc_out.at[pl.ds(4 * k + 2 * h, 2)], f1, f2, g1, g3, f3) for h in range(2)
    ]
    next(step)
    hid[1] = mid[1].finish(0).reshape(16, 8, 256)
    send_a(1, 1, lambda p: hid.at[1, p])
    turn(1, 1)
    for _ in step:
        pass
    end[1].start()
    end[0].pass_on()
    end[1].pass_on()
    end[0].cross()
    end[1].cross()
    o_ref[0:128] = end[0].finish(1)
    o_ref[128:256] = end[1].finish(1)

    for copy in sent:
        copy.wait_send()
    for layer in range(2):
        for h in range(2):
            some = buf_a[layer][h].at[0:15]
            pltpu.make_async_copy(some, some, a_send.at[layer, h]).wait()
            some = send_b.at[layer, h, 0:7]
            pltpu.make_async_copy(some, some, b_send.at[layer, h]).wait()


def shards(features, adjacency_tiles, tile_rows, tile_cols, tile_counts, plan, weights):
    rows, cols, count = tile_rows[0, 0], tile_cols[0, 0], tile_counts[0, 0]
    slots = jnp.arange(256, dtype=jnp.int32)
    place = jnp.where(slots < count, rows * 32 + cols, -1)
    spots = jnp.arange(512, dtype=jnp.int32)
    pos = jnp.min(jnp.where(place[None, :] == spots[:, None], slots[None, :], 256), axis=1)
    piece = (2, 16, 8, 256)
    flat = (2, 2, 8, 8, 256)
    dma = pltpu.SemaphoreType.DMA
    return pl.pallas_call(
        kernel,
        name="graph_layers",
        out_shape=jax.ShapeDtypeStruct((256, 256), F32),
        in_specs=[
            pl.BlockSpec(memory_space=pltpu.SMEM),
            pl.BlockSpec(memory_space=pltpu.SMEM),
            pl.BlockSpec(memory_space=pl.ANY),
            pl.BlockSpec(memory_space=pl.ANY),
            pl.BlockSpec(memory_space=pltpu.VMEM),
        ],
        out_specs=pl.BlockSpec(memory_space=pltpu.VMEM),
        scratch_shapes=[
            pltpu.VMEM((STAGES, GROUP, 128, 128), F32),
            pltpu.VMEM((257, 128, 128), BF),
            pltpu.VMEM((257, 128, 128), BF),
            pltpu.VMEM((2, 2, 2, 16, 8, 8, 256), F32),
            pltpu.VMEM((32, 8, 8, 256), F32),
            pltpu.VMEM((32, 8, 8, 256), F32),
            pltpu.VMEM((16, 8, 256), F32),
            pltpu.VMEM((16, 8, 256), F32),
            pltpu.VMEM((16, 8, 256), F32),
            pltpu.VMEM((16, 8, 256), F32),
            pltpu.VMEM((2, 2, 8, 2, 8, 256), F32),
            pltpu.VMEM((2, 16, 8, 256), F32),
            pltpu.VMEM((256, 256), BF),
            pltpu.VMEM((256, 256), BF),
            pltpu.VMEM((2,) + piece, F32),
            pltpu.VMEM((2, 2) + piece, F32),
            pltpu.VMEM((2,) + piece, F32),
            pltpu.VMEM((2, 16, 8, 256), F32),
            pltpu.VMEM((2, 16, 8, 256), F32),
            pltpu.VMEM((2,) + flat, F32),
            pltpu.VMEM((2, 2) + flat, F32),
            pltpu.VMEM((2,) + flat, F32),
            pltpu.VMEM((2, 2, 8, 8, 256), F32),
            pltpu.VMEM((2, 2, 8, 8, 256), F32),
            dma((STAGES,)),
            dma((COPIES,)),
            dma((COPIES,)),
            dma((2, 2)),
            dma((2, 2)),
            dma((2, 2)),
            dma((2, 2)),
        ],
        compiler_params=pltpu.CompilerParams(
            collective_id=0, has_side_effects=True, vmem_limit_bytes=58 * 2**20
        ),
    )(
        pos,
        plan.reshape(16),
        features.reshape(2, 16, 8, 8, 256),
        adjacency_tiles.reshape(256, 128, 128),
        weights,
    )


def solution(mesh):
    return jax.shard_map(
        shards,
        mesh=mesh,
        in_specs=(
            P("row", None),
            P("row", "rep", None, None, None),
            P("row", "rep", None),
            P("row", "rep", None),
            P("row", "rep"),
            P(),
            P(),
        ),
        out_specs=P(("row", "rep"), None),
        check_vma=False,
    )
```

time: 776 us -> 149 us (0.19)
  waiting for transfers between devices: 478 us -> 0 us
  matrix products: 145 us -> 0 us
  Pallas kernels: 0 us -> 143 us
  local copies, waits for them, and re-layouts: 121 us -> 3.08 us
  between operations: 15.1 us -> 0.66 us
  other arithmetic: 14.9 us -> 1.44 us
    psum x4 -> x0, waiting for transfers between devices: 478 us -> none  [the longest x2 315 us: from_root(): return lax.psum(kept, axis)]
    dot_general x18 -> x0, matrix products: 145 us -> none  [the longest x8 93.9 us: advance(): jnp.einsum('tij,tjf->tif', block_tiles, sources, precision=lax.Precision....]
    pallas_call x0 -> x1, Pallas kernels: none -> 143 us  [shards(): pl.pallas_call(kernel, name='graph_layers', out_shape=jax.ShapeDtypeStruc...]
    while x8 -> x0, local copies, waits for them, and re-layouts: 63.6 us -> none
    gather x8 -> x0, local copies, waits for them, and re-layouts: 52 us -> none  [advance(): sources = jnp.take(received, block_cols, axis=0)]
    dynamic_update_slice x2 -> x0, other arithmetic: 8.92 us -> none  [shards(): lax.dynamic_update_slice_in_dim(received, arrived, section_num * block_le...]
  transfers between devices with their start and end apart: 4 -> 0, of which waited for: 4 -> 0; matrix products, arithmetic and copies ran while one was open for 0% -> 0% of each run, Pallas kernels for 0% -> 0%
where the time goes in v1:
time: 149 us; the launch traced here: 148 us
  Pallas kernels  143 us (96%)
  local copies, waits for them, and re-layouts  3.08 us (2%)
    pallas_call x1, Pallas kernels, shards(): pl.pallas_call(kernel, name='graph_layers', out_shape=jax.ShapeDtypeStruc...  143 us

profile of v1, /device:TPU:0, one launch (start us, length us, event | category | flops | bytes accessed | tf_op | source)
XLA Modules:
  0.0 147.7 jit_solution(520653066695899067)
XLA Ops:
  0.7 0.7 multiply_add_fusion
  1.4 0.7 select_reduce_fusion.pos
  2.1 0.8 copy.10
  2.8 0.7 reshape.27.plan
  3.5 142.5 %graph_layers.1 = f32[256,256]{1,0:T(8,128)} custom-call(s32[512]{0:T(512)} %select_reduce_fusion.pos, s32[16]{0:T(128)} %reshape.27.plan, f32[2,16,8,8,256]{4,3,2,1,0:T(8,128)} %bitcast.6, f32[256,128,128]{2,1,0:T(8,128)} %bitcast.5, f32[2,256,256]{2,1,0:T(8,128)} %w_ref.1), custom_call_target="tpu_custom_call" | custom-call | tf_op jit(solution)/shard_map/graph_layers/pallas_call | solution.py:348
  146.0 1.7 %copy.13 = f32[256,256]{1,0:T(8,128)} copy(f32[256,256]{1,0:T(8,128)} %graph_layers.1) | data formatting | bytes 524288
  (1 shorter events, 0.0 us)

commit v2 on v1

v2 whole, which is shorter than its diff:
```python
import functools

import jax
import jax.numpy as jnp
from jax import lax
from jax.experimental import pallas as pl
from jax.experimental.pallas import tpu as pltpu
from jax.sharding import PartitionSpec as P

BF = jnp.bfloat16
F32 = jnp.float32
MESH = pl.DeviceIdType.MESH
Y, XH, C, XL, Z = 4, 2, 2, 2, 4
GROUP = 16
STAGES = 4
COPIES = 160


def mm(a, b):
    return jnp.dot(a, b, preferred_element_type=F32)


def split(v):
    high = v.astype(BF)
    return high, (v - high.astype(F32)).astype(BF)


def kernel(
    pos, plan, x_ref, tiles, w_ref, o_ref,
    stage, hi, lo, land, acc, acc_out, buf_00, buf_01, buf_10, buf_11, send_b, hid, bh, bl,
    mx, mx_made, mz, mz_made, ex, ex_made, ez, ez_made,
    stage_sem, ssem, rsem, a_send, a_recv, b_send, b_recv,
):
    row, rep = lax.axis_index("row"), lax.axis_index("rep")
    y, xh, c = row // 4, (row // 2) % 2, row % 2
    xl, z = rep // 4, rep % 4

    def rows_dev(dy, dx, dc):
        return ((y + dy) % 4) * 4 + ((xh + dx) % 2) * 2 + (c + dc) % 2

    def reps_dev(dx, dz):
        return ((xl + dx) % 2) * 4 + (z + dz) % 4

    row_peers = [
        rows_dev(a, b, d) for a in range(4) for b in range(2) for d in range(2) if (a, b, d) != (0, 0, 0)
    ]
    rep_peers = [reps_dev(a, b) for a in range(2) for b in range(4) if (a, b) != (0, 0)]

    def load_tiles(g, slot):
        return pltpu.make_async_copy(
            tiles.at[pl.ds(g * GROUP, GROUP)], stage.at[slot], stage_sem.at[slot]
        )

    for g in range(STAGES):
        load_tiles(g, g).start()

    barrier = pltpu.get_barrier_semaphore()
    for peer in row_peers:
        pl.semaphore_signal(barrier, inc=1, device_id=(peer, rep), device_id_type=MESH)
    for peer in rep_peers:
        pl.semaphore_signal(barrier, inc=1, device_id=(row, peer), device_id_type=MESH)
    pl.semaphore_wait(barrier, 22)

    used = [0]
    sent = []

    def remote(src, dst, dev):
        n = used[0]
        used[0] += 1
        copy = pltpu.make_async_remote_copy(
            src_ref=src, dst_ref=dst, send_sem=ssem.at[n], recv_sem=rsem.at[n],
            device_id=dev, device_id_type=MESH,
        )
        sent.append(copy)
        copy.start()
        return copy

    buf_a = ((buf_00, buf_01), (buf_10, buf_11))

    def send_a(layer, h, source):
        for peer in row_peers:
            pltpu.make_async_remote_copy(
                src_ref=source(peer), dst_ref=buf_a[layer][h].at[row],
                send_sem=a_send.at[layer, h], recv_sem=a_recv.at[layer, h],
                device_id=(peer, rep), device_id_type=MESH,
            ).start()
        pltpu.make_async_copy(source(row), buf_a[layer][h].at[row], a_recv.at[layer, h]).start()

    def turn(layer, h):
        whole = buf_a[layer][h]
        pltpu.make_async_copy(whole, whole, a_recv.at[layer, h]).wait()
        for k in range(8):
            for s in range(2):
                send_b[layer, h, k, s] = buf_a[layer][h][plan[k, s]]
        for peer in rep_peers:
            pltpu.make_async_remote_copy(
                src_ref=send_b.at[layer, h, peer], dst_ref=land.at[layer, :, h, row, rep],
                send_sem=b_send.at[layer, h], recv_sem=b_recv.at[layer, h],
                device_id=(row, peer), device_id_type=MESH,
            ).start()
        pltpu.make_async_copy(
            send_b.at[layer, h, rep], land.at[layer, :, h, row, rep], b_recv.at[layer, h]
        ).start()

    def wait_b(layer, h):
        mine = land.at[layer, :, h, row]
        pltpu.make_async_copy(mine, mine, b_recv.at[layer, h]).wait()

    def convert(first, last):
        def one(g, carry):
            slot = lax.rem(g, STAGES)
            load_tiles(g, slot).wait()

            def tile(t, inner):
                high, low = split(stage[slot, t])
                hi[g * GROUP + t] = high
                lo[g * GROUP + t] = low
                return inner

            lax.fori_loop(0, GROUP, tile, 0, unroll=4)

            @pl.when(g + STAGES < 256 // GROUP)
            def _():
                load_tiles(g + STAGES, slot).start()

            return carry

        lax.fori_loop(first, last, one, 0)

    def products(layer, tile_of, count, out, row_tiles):
        def one(j, carry):
            h, q = tile_of(j)
            t = h * 8 + q
            f0 = land[layer, 0, h, pl.ds(q * 2, 2)].reshape(128, 256)
            f1_ = land[layer, 1, h, pl.ds(q * 2, 2)].reshape(128, 256)
            bh[0:128], bl[0:128] = split(f0)
            bh[128:256], bl[128:256] = split(f1_)
            for i in row_tiles:
                a0, a1 = pos[i * 32 + t], pos[i * 32 + 16 + t]
                top = jnp.concatenate([hi[a0], hi[a1]], axis=1)
                low = jnp.concatenate([lo[a0], lo[a1]], axis=1)
                added = mm(top, bh[...]) + mm(top, bl[...]) + mm(low, bh[...])
                out[2 * i : 2 * i + 2] += added.reshape(2, 8, 8, 256)
            return carry

        lax.fori_loop(0, count, one, 0)

    def chip(dy, dx):
        return ((y + dy) % 4) * 2 + (xh + dx) % 2

    def gather_and_multiply(layer, out, rows_of, begin):
        every = range(16)
        core = {}

        def piece(h, dy, dx):
            return land.at[layer, :, h, chip(dy, dx) * 2 + c]

        def half(h, s, dy, dx):
            return land.at[layer, s, h, chip(dy, dx) * 2 + c]

        def move(ref, dy, dx, dc):
            return remote(ref, ref, (rows_dev(dy, dx, dc), rep))

        def share(h, dy, dx):
            core.setdefault((h, dy, dx), []).append(move(piece(h, dy, dx), 0, 0, 1))

        def ready(*keys):
            for key in keys:
                for copy in core[key]:
                    copy.wait_recv()

        def both_ways(h, dx):
            mine = piece(h, 0, dx)
            return move(mine, 1, 0, 0), move(mine, 3, 0, 0)

        far, crossed = {}, {}

        def cross(h, dy):
            crossed[h, dy] = move(piece(h, dy, 0), 0, 1, 0)

        def pass_on(h, dx, pair):
            pair[0].wait_recv()
            a = move(half(h, 0, 3, dx), 1, 0, 0)
            share(h, 3, dx)
            if h == 1:
                cross(h, 3)
            pair[1].wait_recv()
            b = move(half(h, 1, 1, dx), 3, 0, 0)
            share(h, 1, dx)
            if h == 1:
                cross(h, 1)
            far[h, dx] = (a, b)

        def end_far(h, dx):
            for copy in far[h, dx]:
                copy.wait_recv()
            share(h, 2, dx)
            if h == 1:
                cross(h, 2)

        def end_cross(dy):
            crossed[1, dy].wait_recv()
            share(1, dy, 1)

        wait_b(layer, 1)
        along1 = both_ways(1, 0)
        share(1, 0, 0)
        wait_b(layer, 0)
        cross(0, 0)
        along0 = both_ways(0, 0)
        share(0, 0, 0)
        cross(1, 0)
        ready((1, 0, 0), (0, 0, 0))
        products(layer, lambda j: (j, chip(0, 0)), 2, out, every)
        pass_on(1, 0, along1)
        crossed[0, 0].wait_recv()
        along2 = both_ways(0, 1)
        share(0, 0, 1)
        pass_on(0, 0, along0)
        ready((1, 1, 0), (1, 3, 0))
        products(layer, lambda j: (1, chip(1 + 2 * j, 0)), 2, out, every)
        end_far(1, 0)
        end_cross(0)
        ready((0, 0, 1), (0, 1, 0), (0, 3, 0))
        products(layer, lambda j: (0, chip(3 + j, j % 2)), 3, out, every)
        pass_on(0, 1, along2)
        ready((1, 2, 0), (1, 0, 1))
        products(layer, lambda j: (1, chip(2 - 2 * j, j)), 2, out, every)
        end_cross(1)
        end_cross(3)
        ready((0, 1, 1), (0, 3, 1))
        products(layer, lambda j: (0, chip(1 + 2 * j, 1)), 2, out, every)
        end_far(0, 0)
        end_cross(2)
        ready((1, 1, 1), (1, 3, 1))
        products(layer, lambda j: (1, chip(1 + 2 * j, 1)), 2, out, every)
        end_far(0, 1)
        ready((0, 2, 0), (1, 2, 1), (0, 2, 1))
        for h in range(2):
            products(layer, lambda j: (j // 2, chip(2, (j + 1) // 2)), 3, out, rows_of[h])
            begin[h]()

    class ZFirst:
        def __init__(self, part, buf, made):
            self.part, self.buf, self.made = part, buf, made

        def start(self):
            up, down = (row, reps_dev(0, 1)), (row, reps_dev(0, 3))
            part, buf = self.part, self.buf
            self.raw = [
                remote(part((z + 2) % 4), buf.at[0], up),
                remote(part(4 + (z + 2) % 4), buf.at[1], down),
            ]
            self.second = [
                remote(part(4 + (z + 1) % 4), buf.at[3], up),
                remote(part((z + 3) % 4), buf.at[4], down),
            ]

        def pass_on(self):
            up, down = (row, reps_dev(0, 1)), (row, reps_dev(0, 3))
            buf, made = self.buf, self.made
            self.raw[0].wait_recv()
            made[0] = self.part((z + 1) % 4)[...] + buf[0]
            self.second.append(remote(made.at[0], buf.at[2], up))
            self.raw[1].wait_recv()
            made[1] = self.part(4 + (z + 3) % 4)[...] + buf[1]
            self.second.append(remote(made.at[1], buf.at[5], down))

        def cross(self):
            for copy in self.second:
                copy.wait_recv()
            other, buf = 1 - xl, self.buf
            self.made[2] = self.part(other * 4 + z)[...] + buf[2 + other] + buf[4 + other]
            self.last = remote(self.made.at[2], buf.at[6], (row, reps_dev(1, 0)))

        def total(self):
            buf = self.buf
            mine = self.part(rep)[...] + buf[2 + xl] + buf[4 + xl]
            self.last.wait_recv()
            return mine + buf[6]

    class XFirst:
        def __init__(self, part, buf, made):
            self.part, self.buf, self.made = part, buf, made
            self.n = made.shape[1] // 2

        def start(self):
            over = (row, reps_dev(1, 0))
            self.over = {
                b: remote(self.part(reps_dev(1, b)), self.buf.at[b], over) for b in (2, 1, 3, 0)
            }

        def near(self, b):
            self.over[b].wait_recv()
            return self.part(reps_dev(0, b))[...] + self.buf[b]

        def halves(self, ref):
            return ref.at[pl.ds(0, self.n)], ref.at[pl.ds(self.n, self.n)]

        def send_far(self):
            up, down = (row, reps_dev(0, 1)), (row, reps_dev(0, 3))
            made, buf = self.made, self.buf
            made[0] = self.near(2)
            (m0, m1), (b0, b1) = self.halves(made.at[0]), self.halves(buf.at[4])
            self.far = [remote(m0, b0, up), remote(m1, b1, down)]

        def send_near(self):
            up, down = (row, reps_dev(0, 1)), (row, reps_dev(0, 3))
            made, buf = self.made, self.buf
            made[1] = self.near(1)
            self.up, self.up_to = self.halves(made.at[1]), self.halves(buf.at[5])
            self.last = [remote(self.up[1], self.up_to[1], up)]
            made[2] = self.near(3)
            self.down, self.down_to = self.halves(made.at[2]), self.halves(buf.at[6])
            self.last.append(remote(self.down[0], self.down_to[0], down))

        def pass_on(self):
            up, down = (row, reps_dev(0, 1)), (row, reps_dev(0, 3))
            n, made, buf = self.n, self.made, self.buf
            self.far[0].wait_recv()
            made[1, 0:n] += buf[4, 0:n]
            self.last.append(remote(self.up[0], self.up_to[0], up))
            self.far[1].wait_recv()
            made[2, n:] += buf[4, n:]
            self.last.append(remote(self.down[1], self.down_to[1], down))

        def total(self):
            mine = self.near(0)
            for copy in self.last:
                copy.wait_recv()
            return mine + self.buf[5] + self.buf[6]

    def transform(total, layer):
        wh, wl = split(w_ref[layer])
        th, tl = split(total.reshape(128, 256))
        return jnp.maximum(mm(th, wh) + mm(th, wl) + mm(tl, wh), 0.0)

    def add_up(x_first, z_first, use):
        z_first.pass_on()
        x_first.send_far()
        z_first.cross()
        x_first.send_near()
        x_first.pass_on()
        use(1, z_first.total())
        use(0, x_first.total())

    for h in (1, 0):
        send_a(0, h, lambda p, h=h: x_ref.at[h, p, rep])
    hi[256] = jnp.zeros((128, 128), BF)
    lo[256] = jnp.zeros((128, 128), BF)

    def clear(i, carry):
        acc[i] = jnp.zeros((8, 8, 256), F32)
        acc_out[i] = jnp.zeros((8, 8, 256), F32)
        return carry

    lax.fori_loop(0, 32, clear, 0)
    convert(0, 6)
    turn(0, 1)
    turn(0, 0)
    convert(6, 256 // GROUP)

    def mid_part(h):
        return lambda k: acc.at[pl.ds(16 * h, 16), k]

    def end_part(h):
        return lambda k: acc_out.at[pl.ds(4 * k + 2 * h, 2)]

    mid = XFirst(mid_part(0), mx, mx_made), ZFirst(mid_part(1), mz, mz_made)
    end = XFirst(end_part(0), ex, ex_made), ZFirst(end_part(1), ez, ez_made)

    gather_and_multiply(
        0, acc, (range(8), range(8, 16)), (mid[0].start, mid[1].start)
    )

    def use_mid(h, total):
        hid[h] = transform(total, 0).reshape(16, 8, 256)
        send_a(1, h, lambda p: hid.at[h, p])

    add_up(*mid, use_mid)
    turn(1, 1)
    turn(1, 0)
    gather_and_multiply(
        1, acc_out, (range(0, 16, 2), range(1, 16, 2)), (end[0].start, end[1].start)
    )

    def use_end(h, total):
        o_ref[128 * h : 128 * h + 128] = transform(total, 1)

    add_up(*end, use_end)

    for copy in sent:
        copy.wait_send()
    for layer in range(2):
        for h in range(2):
            some = buf_a[layer][h].at[0:15]
            pltpu.make_async_copy(some, some, a_send.at[layer, h]).wait()
            some = send_b.at[layer, h, 0:7]
            pltpu.make_async_copy(some, some, b_send.at[layer, h]).wait()


def shards(features, adjacency_tiles, tile_rows, tile_cols, tile_counts, plan, weights):
    rows, cols, count = tile_rows[0, 0], tile_cols[0, 0], tile_counts[0, 0]
    slots = jnp.arange(256, dtype=jnp.int32)
    place = jnp.where(slots < count, rows * 32 + cols, -1)
    spots = jnp.arange(512, dtype=jnp.int32)
    pos = jnp.min(jnp.where(place[None, :] == spots[:, None], slots[None, :], 256), axis=1)
    piece = (16, 8, 256)
    flat = (2, 8, 8, 256)
    dma = pltpu.SemaphoreType.DMA
    return pl.pallas_call(
        kernel,
        name="graph_layers",
        out_shape=jax.ShapeDtypeStruct((256, 256), F32),
        in_specs=[
            pl.BlockSpec(memory_space=pltpu.SMEM),
            pl.BlockSpec(memory_space=pltpu.SMEM),
            pl.BlockSpec(memory_space=pl.ANY),
            pl.BlockSpec(memory_space=pl.ANY),
            pl.BlockSpec(memory_space=pltpu.VMEM),
        ],
        out_specs=pl.BlockSpec(memory_space=pltpu.VMEM),
        scratch_shapes=[
            pltpu.VMEM((STAGES, GROUP, 128, 128), F32),
            pltpu.VMEM((257, 128, 128), BF),
            pltpu.VMEM((257, 128, 128), BF),
            pltpu.VMEM((2, 2, 2, 16, 8, 8, 256), F32),
            pltpu.VMEM((32, 8, 8, 256), F32),
            pltpu.VMEM((32, 8, 8, 256), F32),
            pltpu.VMEM((16, 8, 256), F32),
            pltpu.VMEM((16, 8, 256), F32),
            pltpu.VMEM((16, 8, 256), F32),
            pltpu.VMEM((16, 8, 256), F32),
            pltpu.VMEM((2, 2, 8, 2, 8, 256), F32),
            pltpu.VMEM((2, 16, 8, 256), F32),
            pltpu.VMEM((256, 256), BF),
            pltpu.VMEM((256, 256), BF),
            pltpu.VMEM((7,) + piece, F32),
            pltpu.VMEM((3,) + piece, F32),
            pltpu.VMEM((7,) + piece, F32),
            pltpu.VMEM((3,) + piece, F32),
            pltpu.VMEM((7,) + flat, F32),
            pltpu.VMEM((3,) + flat, F32),
            pltpu.VMEM((7,) + flat, F32),
            pltpu.VMEM((3,) + flat, F32),
            dma((STAGES,)),
            dma((COPIES,)),
            dma((COPIES,)),
            dma((2, 2)),
            dma((2, 2)),
            dma((2, 2)),
            dma((2, 2)),
        ],
        compiler_params=pltpu.CompilerParams(
            collective_id=0, has_side_effects=True, vmem_limit_bytes=58 * 2**20
        ),
    )(
        pos,
        plan,
        features.reshape(2, 16, 8, 8, 256),
        adjacency_tiles.reshape(256, 128, 128),
        weights,
    )


def solution(mesh):
    return jax.shard_map(
        shards,
        mesh=mesh,
        in_specs=(
            P("row", None),
            P("row", "rep", None, None, None),
            P("row", "rep", None),
            P("row", "rep", None),
            P("row", "rep"),
            P(),
            P(),
        ),
        out_specs=P(("row", "rep"), None),
        check_vma=False,
    )
```

time: 149 us -> 122 us (0.82)
  Pallas kernels: 143 us -> 115 us
    pallas_call x1, Pallas kernels: 143 us -> 115 us  [shards(): pl.pallas_call(kernel, name='graph_layers', out_shape=jax.ShapeDtypeStruc...]
where the time goes in v2:
time: 122 us; the launch traced here: 120 us
  Pallas kernels  115 us (94%)
  local copies, waits for them, and re-layouts  3.01 us (2%)
  other arithmetic  1.43 us (1%)
    pallas_call x1, Pallas kernels, shards(): pl.pallas_call(kernel, name='graph_layers', out_shape=jax.ShapeDtypeStruc...  115 us
    unnamed x2, local copies, waits for them, and re-layouts  3.01 us

profile of v2, /device:TPU:0, one launch (start us, length us, event | category | flops | bytes accessed | tf_op | source)
XLA Modules:
  0.0 120.4 jit_solution(7704773240770877312)
XLA Ops:
  0.7 0.7 multiply_add_fusion
  1.4 0.7 select_reduce_fusion.pos
  2.1 1.3 %copy.9.plan = s32[8,2]{1,0:T(8,128)} copy(s32[8,2]{0,1:T(2,128)} %param.12) | data formatting | bytes 128 | tf_op args[5]
  3.4 115.3 %graph_layers.1 = f32[256,256]{1,0:T(8,128)} custom-call(s32[512]{0:T(512)} %select_reduce_fusion.pos, s32[8,2]{1,0:T(8,128)} %copy.9.plan, f32[2,16,8,8,256]{4,3,2,1,0:T(8,128)} %bitcast.6, f32[256,128,128]{2,1,0:T(8,128)} %bitcast.5, f32[2,256,256]{2,1,0:T(8,128)} %w_ref.1), custom_call_target="tpu_custom_call" | custom-call | tf_op jit(solution)/shard_map/graph_layers/pallas_call | solution.py:411
  118.8 1.7 %copy.12 = f32[256,256]{1,0:T(8,128)} copy(f32[256,256]{1,0:T(8,128)} %graph_layers.1) | data formatting | bytes 524288
  (1 shorter events, 0.0 us)

commit v3 on v2

--- a/solution.py
+++ b/solution.py
@@ -26,10 +26,10 @@
 
 
 def kernel(
-    pos, plan, x_ref, tiles, w_ref, o_ref,
-    stage, hi, lo, land, acc, acc_out, buf_00, buf_01, buf_10, buf_11, send_b, hid, bh, bl,
+    rows_ref, cols_ref, count_ref, plan_ref, x_ref, tiles, w_ref, o_ref,
+    stage, hi, lo, land, acc, acc_out, big_0, big_1, send_b, hid, bh, bl, w_high, w_low,
     mx, mx_made, mz, mz_made, ex, ex_made, ez, ez_made,
-    stage_sem, ssem, rsem, a_send, a_recv, b_send, b_recv,
+    pos_made, pos, plan, pos_sem, plan_sem, stage_sem, ssem, rsem, a_send, a_recv, b_send, b_recv,
 ):
     row, rep = lax.axis_index("row"), lax.axis_index("rep")
     y, xh, c = row // 4, (row // 2) % 2, row % 2
@@ -41,10 +41,12 @@
     def reps_dev(dx, dz):
         return ((xl + dx) % 2) * 4 + (z + dz) % 4
 
-    row_peers = [
-        rows_dev(a, b, d) for a in range(4) for b in range(2) for d in range(2) if (a, b, d) != (0, 0, 0)
+    plane = [(2, 1), (2, 0), (1, 1), (3, 1), (0, 1), (1, 0), (3, 0)]
+    row_peers = [rows_dev(a, b, 0) for a, b in plane]
+    near_peers = [(rows_dev(a, b, 0), reps_dev(b, 0)) for a, b in plane]
+    rep_peers = [
+        reps_dev(a, b) for a, b in ((1, 2), (0, 2), (1, 1), (1, 3), (1, 0), (0, 1), (0, 3))
     ]
-    rep_peers = [reps_dev(a, b) for a in range(2) for b in range(4) if (a, b) != (0, 0)]
 
     def load_tiles(g, slot):
         return pltpu.make_async_copy(
@@ -54,12 +56,17 @@
     for g in range(STAGES):
         load_tiles(g, g).start()
 
+    fetch_plan = pltpu.make_async_copy(plan_ref, plan, plan_sem)
+    fetch_plan.start()
     barrier = pltpu.get_barrier_semaphore()
-    for peer in row_peers:
+    for peer in row_peers + [rows_dev(0, 0, 1)]:
         pl.semaphore_signal(barrier, inc=1, device_id=(peer, rep), device_id_type=MESH)
     for peer in rep_peers:
         pl.semaphore_signal(barrier, inc=1, device_id=(row, peer), device_id_type=MESH)
-    pl.semaphore_wait(barrier, 22)
+    for (_, b), (peer, to) in zip(plane, near_peers):
+        if b:
+            pl.semaphore_signal(barrier, inc=1, device_id=(peer, to), device_id_type=MESH)
+    pl.semaphore_wait(barrier, 19)
 
     used = [0]
     sent = []
@@ -75,36 +82,57 @@
         copy.start()
         return copy
 
-    buf_a = ((buf_00, buf_01), (buf_10, buf_11))
-
-    def send_a(layer, h, source):
-        for peer in row_peers:
+    big = (big_0, big_1)
+    here = row // 2
+
+    def send_a(layer, source, peers):
+        for peer, to in peers:
             pltpu.make_async_remote_copy(
-                src_ref=source(peer), dst_ref=buf_a[layer][h].at[row],
-                send_sem=a_send.at[layer, h], recv_sem=a_recv.at[layer, h],
-                device_id=(peer, rep), device_id_type=MESH,
+                src_ref=source(peer // 2, to), dst_ref=big[layer].at[here, c],
+                send_sem=a_send.at[layer], recv_sem=a_recv.at[layer],
+                device_id=(peer, to), device_id_type=MESH,
             ).start()
-        pltpu.make_async_copy(source(row), buf_a[layer][h].at[row], a_recv.at[layer, h]).start()
-
-    def turn(layer, h):
-        whole = buf_a[layer][h]
-        pltpu.make_async_copy(whole, whole, a_recv.at[layer, h]).wait()
-        for k in range(8):
-            for s in range(2):
-                send_b[layer, h, k, s] = buf_a[layer][h][plan[k, s]]
-        for peer in rep_peers:
-            pltpu.make_async_remote_copy(
-                src_ref=send_b.at[layer, h, peer], dst_ref=land.at[layer, :, h, row, rep],
-                send_sem=b_send.at[layer, h], recv_sem=b_recv.at[layer, h],
-                device_id=(row, peer), device_id_type=MESH,
+        pltpu.make_async_copy(source(here, rep), big[layer].at[here, c], a_recv.at[layer]).start()
+
+    def turn(layer):
+        plane_part = big[layer].at[:, c]
+        pltpu.make_async_copy(plane_part, plane_part, a_recv.at[layer]).wait()
+        other = big[layer].at[:, c, :, 1 - c]
+        remote(other, other, (rows_dev(0, 0, 1), rep)).wait_recv()
+        for h in (1, 0):
+            for k in range(8):
+                for s in range(2):
+                    r = plan[s, k]
+                    send_b[layer, h, k, s] = big[layer][r // 2, r % 2, h, c]
+            for peer in rep_peers:
+                pltpu.make_async_remote_copy(
+                    src_ref=send_b.at[layer, h, peer], dst_ref=land.at[layer, :, h, row, rep],
+                    send_sem=b_send.at[layer, h], recv_sem=b_recv.at[layer, h],
+                    device_id=(row, peer), device_id_type=MESH,
+                ).start()
+            pltpu.make_async_copy(
+                send_b.at[layer, h, rep], land.at[layer, :, h, row, rep], b_recv.at[layer, h]
             ).start()
-        pltpu.make_async_copy(
-            send_b.at[layer, h, rep], land.at[layer, :, h, row, rep], b_recv.at[layer, h]
-        ).start()
 
     def wait_b(layer, h):
         mine = land.at[layer, :, h, row]
         pltpu.make_async_copy(mine, mine, b_recv.at[layer, h]).wait()
+
+    def place_tiles():
+        slot = lax.broadcasted_iota(jnp.int32, (1, 256), 1)
+        key = jnp.where(slot < count_ref[0, 0], rows_ref[...] * 32 + cols_ref[...], -1)
+        down = lax.broadcasted_iota(jnp.int32, (128, 128), 0)
+        spot = lax.broadcasted_iota(jnp.int32, (128, 128), 1)
+        keys = [
+            jnp.broadcast_to(key[:, 128 * n : 128 * n + 128], (128, 128)).T for n in range(2)
+        ]
+        for b in range(4):
+            found = jnp.minimum(
+                jnp.where(keys[0] == spot + 128 * b, down, 256),
+                jnp.where(keys[1] == spot + 128 * b, down + 128, 256),
+            )
+            pos_made[b : b + 1] = jnp.min(found, axis=0, keepdims=True)
+        pltpu.make_async_copy(pos_made, pos, pos_sem).start()
 
     def convert(first, last):
         def one(g, carry):
@@ -136,7 +164,7 @@
             bh[0:128], bl[0:128] = split(f0)
             bh[128:256], bl[128:256] = split(f1_)
             for i in row_tiles:
-                a0, a1 = pos[i * 32 + t], pos[i * 32 + 16 + t]
+                a0, a1 = pos[i // 4, i % 4 * 32 + t], pos[i // 4, i % 4 * 32 + 16 + t]
                 top = jnp.concatenate([hi[a0], hi[a1]], axis=1)
                 low = jnp.concatenate([lo[a0], lo[a1]], axis=1)
                 added = mm(top, bh[...]) + mm(top, bl[...]) + mm(low, bh[...])
@@ -331,9 +359,9 @@
             return mine + self.buf[5] + self.buf[6]
 
     def transform(total, layer):
-        wh, wl = split(w_ref[layer])
+        wh, wl = w_high[layer], w_low[layer]
         th, tl = split(total.reshape(128, 256))
-        return jnp.maximum(mm(th, wh) + mm(th, wl) + mm(tl, wh), 0.0)
+        return mm(th, wh) + mm(th, wl) + mm(tl, wh)
 
     def add_up(x_first, z_first, use):
         z_first.pass_on()
@@ -344,8 +372,10 @@
         use(1, z_first.total())
         use(0, x_first.total())
 
-    for h in (1, 0):
-        send_a(0, h, lambda p, h=h: x_ref.at[h, p, rep])
+    send_a(0, lambda q, k: x_ref.at[:, pl.ds(2 * q, 2), k], near_peers)
+    place_tiles()
+    for layer in range(2):
+        w_high[layer], w_low[layer] = split(w_ref[layer])
     hi[256] = jnp.zeros((128, 128), BF)
     lo[256] = jnp.zeros((128, 128), BF)
 
@@ -355,10 +385,11 @@
         return carry
 
     lax.fori_loop(0, 32, clear, 0)
-    convert(0, 6)
-    turn(0, 1)
-    turn(0, 0)
-    convert(6, 256 // GROUP)
+    convert(0, 4)
+    fetch_plan.wait()
+    turn(0)
+    convert(4, 256 // GROUP)
+    pltpu.make_async_copy(pos_made, pos, pos_sem).wait()
 
     def mid_part(h):
         return lambda k: acc.at[pl.ds(16 * h, 16), k]
@@ -374,12 +405,11 @@
     )
 
     def use_mid(h, total):
-        hid[h] = transform(total, 0).reshape(16, 8, 256)
-        send_a(1, h, lambda p: hid.at[h, p])
+        hid[h] = jnp.maximum(transform(total, 0), 0.0).reshape(16, 8, 256)
 
     add_up(*mid, use_mid)
-    turn(1, 1)
-    turn(1, 0)
+    send_a(1, lambda q, k: hid.at[:, pl.ds(2 * q, 2)], [(peer, rep) for peer in row_peers])
+    turn(1)
     gather_and_multiply(
         1, acc_out, (range(0, 16, 2), range(1, 16, 2)), (end[0].start, end[1].start)
     )
@@ -392,29 +422,26 @@
     for copy in sent:
         copy.wait_send()
     for layer in range(2):
+        some = big[layer].at[0:7, 0]
+        pltpu.make_async_copy(some, some, a_send.at[layer]).wait()
         for h in range(2):
-            some = buf_a[layer][h].at[0:15]
-            pltpu.make_async_copy(some, some, a_send.at[layer, h]).wait()
             some = send_b.at[layer, h, 0:7]
             pltpu.make_async_copy(some, some, b_send.at[layer, h]).wait()
 
 
 def shards(features, adjacency_tiles, tile_rows, tile_cols, tile_counts, plan, weights):
-    rows, cols, count = tile_rows[0, 0], tile_cols[0, 0], tile_counts[0, 0]
-    slots = jnp.arange(256, dtype=jnp.int32)
-    place = jnp.where(slots < count, rows * 32 + cols, -1)
-    spots = jnp.arange(512, dtype=jnp.int32)
-    pos = jnp.min(jnp.where(place[None, :] == spots[:, None], slots[None, :], 256), axis=1)
     piece = (16, 8, 256)
     flat = (2, 8, 8, 256)
     dma = pltpu.SemaphoreType.DMA
-    return pl.pallas_call(
+    product = pl.pallas_call(
         kernel,
         name="graph_layers",
         out_shape=jax.ShapeDtypeStruct((256, 256), F32),
         in_specs=[
+            pl.BlockSpec(memory_space=pltpu.VMEM),
+            pl.BlockSpec(memory_space=pltpu.VMEM),
             pl.BlockSpec(memory_space=pltpu.SMEM),
-            pl.BlockSpec(memory_space=pltpu.SMEM),
+            pl.BlockSpec(memory_space=pl.ANY),
             pl.BlockSpec(memory_space=pl.ANY),
             pl.BlockSpec(memory_space=pl.ANY),
             pl.BlockSpec(memory_space=pltpu.VMEM),
@@ -427,14 +454,14 @@
             pltpu.VMEM((2, 2, 2, 16, 8, 8, 256), F32),
             pltpu.VMEM((32, 8, 8, 256), F32),
             pltpu.VMEM((32, 8, 8, 256), F32),
-            pltpu.VMEM((16, 8, 256), F32),
-            pltpu.VMEM((16, 8, 256), F32),
-            pltpu.VMEM((16, 8, 256), F32),
-            pltpu.VMEM((16, 8, 256), F32),
+            pltpu.VMEM((8, 2, 2, 2, 8, 256), F32),
+            pltpu.VMEM((8, 2, 2, 2, 8, 256), F32),
             pltpu.VMEM((2, 2, 8, 2, 8, 256), F32),
             pltpu.VMEM((2, 16, 8, 256), F32),
             pltpu.VMEM((256, 256), BF),
             pltpu.VMEM((256, 256), BF),
+            pltpu.VMEM((2, 256, 256), BF),
+            pltpu.VMEM((2, 256, 256), BF),
             pltpu.VMEM((7,) + piece, F32),
             pltpu.VMEM((3,) + piece, F32),
             pltpu.VMEM((7,) + piece, F32),
@@ -443,11 +470,16 @@
             pltpu.VMEM((3,) + flat, F32),
             pltpu.VMEM((7,) + flat, F32),
             pltpu.VMEM((3,) + flat, F32),
+            pltpu.VMEM((4, 128), jnp.int32),
+            pltpu.SMEM((4, 128), jnp.int32),
+            pltpu.SMEM((2, 8), jnp.int32),
+            dma,
+            dma,
             dma((STAGES,)),
             dma((COPIES,)),
             dma((COPIES,)),
-            dma((2, 2)),
-            dma((2, 2)),
+            dma((2,)),
+            dma((2,)),
             dma((2, 2)),
             dma((2, 2)),
         ],
@@ -455,12 +487,15 @@
             collective_id=0, has_side_effects=True, vmem_limit_bytes=58 * 2**20
         ),
     )(
-        pos,
-        plan,
+        tile_rows.reshape(1, 256),
+        tile_cols.reshape(1, 256),
+        tile_counts,
+        plan.T,
         features.reshape(2, 16, 8, 8, 256),
         adjacency_tiles.reshape(256, 128, 128),
         weights,
     )
+    return jnp.maximum(product, 0.0)
 
 
 def solution(mesh):

time: 122 us -> 119 us (0.975)
  local copies, waits for them, and re-layouts: 3.01 us -> 0 us
    unnamed x2 -> x0, local copies, waits for them, and re-layouts: 3.01 us -> none
    max x0 -> x1, other arithmetic: none -> 1.67 us  [shards(): return jnp.maximum(product, 0.0)]
where the time goes in v3:
time: 119 us; the launch traced here: 118 us
  Pallas kernels  116 us (97%)
  other arithmetic  1.67 us (1%)
    pallas_call x1, Pallas kernels, shards(): pl.pallas_call(kernel, name='graph_layers', out_shape=jax.ShapeDtypeStruc...  116 us

profile of v3, /device:TPU:0, one launch (start us, length us, event | category | flops | bytes accessed | tf_op | source)
XLA Modules:
  0.0 118.4 jit_solution(7336073858390203055)
XLA Ops:
  0.7 116.1 %graph_layers.1 = f32[256,256]{1,0:T(8,128)} custom-call(s32[1,256]{1,0:T(1,128)} %bitcast.7, s32[1,256]{1,0:T(1,128)} %bitcast.8, s32[1,1]{1,0:T(1,128)S(6)} %copy.8.count_ref, s32[2,8]{1,0:T(2,128)} %bitcast.9, f32[2,16,8,8,256]{4,3,2,1,0:T(8,128)} %bitcast.6, f32[256,128,128]{2,1,0:T(8,128)} %bitcast.5, f32[2,256,256]{2,1,0:T(8,128)} %w_ref.1), custom_call_target="tpu_custom_call" | custom-call | tf_op jit(solution)/shard_map/graph_layers/pallas_call | solution.py:436
  116.7 1.7 %broadcast_maximum_fusion = f32[256,256]{1,0:T(8,128)} fusion(f32[256,256]{1,0:T(8,128)} %graph_layers.1), kind=kLoop, calls=%fused_computation | loop fusion | flops 65536 | bytes 524288 | tf_op jit(solution)/shard_map/max | solution.py:498

commit v4 on v3

--- a/solution.py
+++ b/solution.py
@@ -27,7 +27,7 @@
 
 def kernel(
     rows_ref, cols_ref, count_ref, plan_ref, x_ref, tiles, w_ref, o_ref,
-    stage, hi, lo, land, acc, acc_out, big_0, big_1, send_b, hid, bh, bl, w_high, w_low,
+    stage, hi, lo, land, acc, acc_out, big_0, big_10, big_11, send_b, hid, bh, bl, w_high, w_low,
     mx, mx_made, mz, mz_made, ex, ex_made, ez, ez_made,
     pos_made, pos, plan, pos_sem, plan_sem, stage_sem, ssem, rsem, a_send, a_recv, b_send, b_recv,
 ):
@@ -82,28 +82,28 @@
         copy.start()
         return copy
 
-    big = (big_0, big_1)
+    big = (big_0, big_10, big_11)
     here = row // 2
 
-    def send_a(layer, source, peers):
+    def send_a(n, source, peers):
         for peer, to in peers:
             pltpu.make_async_remote_copy(
-                src_ref=source(peer // 2, to), dst_ref=big[layer].at[here, c],
-                send_sem=a_send.at[layer], recv_sem=a_recv.at[layer],
+                src_ref=source(peer // 2, to), dst_ref=big[n].at[here, c],
+                send_sem=a_send.at[n], recv_sem=a_recv.at[n],
                 device_id=(peer, to), device_id_type=MESH,
             ).start()
-        pltpu.make_async_copy(source(here, rep), big[layer].at[here, c], a_recv.at[layer]).start()
-
-    def turn(layer):
-        plane_part = big[layer].at[:, c]
-        pltpu.make_async_copy(plane_part, plane_part, a_recv.at[layer]).wait()
-        other = big[layer].at[:, c, :, 1 - c]
+        pltpu.make_async_copy(source(here, rep), big[n].at[here, c], a_recv.at[n]).start()
+
+    def turn(layer, n, chunks):
+        plane_part = big[n].at[:, c]
+        pltpu.make_async_copy(plane_part, plane_part, a_recv.at[n]).wait()
+        other = big[n].at[:, c, :, 1 - c]
         remote(other, other, (rows_dev(0, 0, 1), rep)).wait_recv()
-        for h in (1, 0):
+        for at, h in chunks:
             for k in range(8):
                 for s in range(2):
                     r = plan[s, k]
-                    send_b[layer, h, k, s] = big[layer][r // 2, r % 2, h, c]
+                    send_b[layer, h, k, s] = big[n][r // 2, r % 2, at, c]
             for peer in rep_peers:
                 pltpu.make_async_remote_copy(
                     src_ref=send_b.at[layer, h, peer], dst_ref=land.at[layer, :, h, row, rep],
@@ -155,23 +155,25 @@
 
         lax.fori_loop(first, last, one, 0)
 
-    def products(layer, tile_of, count, out, row_tiles):
-        def one(j, carry):
-            h, q = tile_of(j)
-            t = h * 8 + q
-            f0 = land[layer, 0, h, pl.ds(q * 2, 2)].reshape(128, 256)
-            f1_ = land[layer, 1, h, pl.ds(q * 2, 2)].reshape(128, 256)
-            bh[0:128], bl[0:128] = split(f0)
-            bh[128:256], bl[128:256] = split(f1_)
-            for i in row_tiles:
+    def products(layer, chips, out, row_tiles, fresh=True):
+        right = []
+        for n, (h, q) in enumerate(chips):
+            if fresh:
+                for s in range(2):
+                    part = land[layer, s, h, pl.ds(q * 2, 2)].reshape(128, 256)
+                    r = slice(128 * s, 128 * s + 128)
+                    bh[n, r], bl[n, r] = split(part)
+            right += [bh[n], bh[n], bl[n]]
+        right = jnp.concatenate(right, axis=0)
+        for i in row_tiles:
+            left = []
+            for h, q in chips:
+                t = h * 8 + q
                 a0, a1 = pos[i // 4, i % 4 * 32 + t], pos[i // 4, i % 4 * 32 + 16 + t]
-                top = jnp.concatenate([hi[a0], hi[a1]], axis=1)
-                low = jnp.concatenate([lo[a0], lo[a1]], axis=1)
-                added = mm(top, bh[...]) + mm(top, bl[...]) + mm(low, bh[...])
-                out[2 * i : 2 * i + 2] += added.reshape(2, 8, 8, 256)
-            return carry
-
-        lax.fori_loop(0, count, one, 0)
+                top0, top1 = hi[a0], hi[a1]
+                left += [top0, top1, lo[a0], lo[a1], top0, top1]
+            added = mm(jnp.concatenate(left, axis=1), right)
+            out[2 * i : 2 * i + 2] += added.reshape(2, 8, 8, 256)
 
     def chip(dy, dx):
         return ((y + dy) % 4) * 2 + (xh + dx) % 2
@@ -239,33 +241,35 @@
         share(0, 0, 0)
         cross(1, 0)
         ready((1, 0, 0), (0, 0, 0))
-        products(layer, lambda j: (j, chip(0, 0)), 2, out, every)
+        products(layer, [(0, chip(0, 0)), (1, chip(0, 0))], out, every)
         pass_on(1, 0, along1)
         crossed[0, 0].wait_recv()
         along2 = both_ways(0, 1)
         share(0, 0, 1)
         pass_on(0, 0, along0)
         ready((1, 1, 0), (1, 3, 0))
-        products(layer, lambda j: (1, chip(1 + 2 * j, 0)), 2, out, every)
+        products(layer, [(1, chip(1, 0)), (1, chip(3, 0))], out, every)
         end_far(1, 0)
         end_cross(0)
-        ready((0, 0, 1), (0, 1, 0), (0, 3, 0))
-        products(layer, lambda j: (0, chip(3 + j, j % 2)), 3, out, every)
+        ready((0, 0, 1), (0, 3, 0))
+        products(layer, [(0, chip(3, 0)), (0, chip(0, 1))], out, every)
         pass_on(0, 1, along2)
-        ready((1, 2, 0), (1, 0, 1))
-        products(layer, lambda j: (1, chip(2 - 2 * j, j)), 2, out, every)
+        ready((0, 1, 0), (1, 2, 0), (1, 0, 1))
+        products(layer, [(0, chip(1, 0)), (1, chip(2, 0)), (1, chip(0, 1))], out, every)
         end_cross(1)
         end_cross(3)
+        end_far(0, 0)
         ready((0, 1, 1), (0, 3, 1))
-        products(layer, lambda j: (0, chip(1 + 2 * j, 1)), 2, out, every)
-        end_far(0, 0)
+        products(layer, [(0, chip(1, 1)), (0, chip(3, 1))], out, every)
         end_cross(2)
-        ready((1, 1, 1), (1, 3, 1))
-        products(layer, lambda j: (1, chip(1 + 2 * j, 1)), 2, out, every)
+        ready((1, 1, 1), (1, 3, 1), (0, 2, 0))
+        products(layer, [(1, chip(1, 1)), (1, chip(3, 1)), (0, chip(2, 0))], out, every)
         end_far(0, 1)
-        ready((0, 2, 0), (1, 2, 1), (0, 2, 1))
+        ready((1, 2, 1), (0, 2, 1))
         for h in range(2):
-            products(layer, lambda j: (j // 2, chip(2, (j + 1) // 2)), 3, out, rows_of[h])
+            products(
+                layer, [(0, chip(2, 1)), (1, chip(2, 1))], out, rows_of[h], h == 0
+            )
             begin[h]()
 
     class ZFirst:
@@ -387,7 +391,7 @@
     lax.fori_loop(0, 32, clear, 0)
     convert(0, 4)
     fetch_plan.wait()
-    turn(0)
+    turn(0, 0, ((1, 1), (0, 0)))
     convert(4, 256 // GROUP)
     pltpu.make_async_copy(pos_made, pos, pos_sem).wait()
 
@@ -406,10 +410,15 @@
 
     def use_mid(h, total):
         hid[h] = jnp.maximum(transform(total, 0), 0.0).reshape(16, 8, 256)
+        send_a(
+            1 + h,
+            lambda q, k: hid.at[pl.ds(h, 1), pl.ds(2 * q, 2)],
+            [(peer, rep) for peer in row_peers],
+        )
 
     add_up(*mid, use_mid)
-    send_a(1, lambda q, k: hid.at[:, pl.ds(2 * q, 2)], [(peer, rep) for peer in row_peers])
-    turn(1)
+    turn(1, 2, ((0, 1),))
+    turn(1, 1, ((0, 0),))
     gather_and_multiply(
         1, acc_out, (range(0, 16, 2), range(1, 16, 2)), (end[0].start, end[1].start)
     )
@@ -421,9 +430,10 @@
 
     for copy in sent:
         copy.wait_send()
+    for n in range(3):
+        some = big[n].at[0:7, 0]
+        pltpu.make_async_copy(some, some, a_send.at[n]).wait()
     for layer in range(2):
-        some = big[layer].at[0:7, 0]
-        pltpu.make_async_copy(some, some, a_send.at[layer]).wait()
         for h in range(2):
             some = send_b.at[layer, h, 0:7]
             pltpu.make_async_copy(some, some, b_send.at[layer, h]).wait()
@@ -455,11 +465,12 @@
             pltpu.VMEM((32, 8, 8, 256), F32),
             pltpu.VMEM((32, 8, 8, 256), F32),
             pltpu.VMEM((8, 2, 2, 2, 8, 256), F32),
-            pltpu.VMEM((8, 2, 2, 2, 8, 256), F32),
+            pltpu.VMEM((8, 2, 1, 2, 8, 256), F32),
+            pltpu.VMEM((8, 2, 1, 2, 8, 256), F32),
             pltpu.VMEM((2, 2, 8, 2, 8, 256), F32),
             pltpu.VMEM((2, 16, 8, 256), F32),
-            pltpu.VMEM((256, 256), BF),
-            pltpu.VMEM((256, 256), BF),
+            pltpu.VMEM((3, 256, 256), BF),
+            pltpu.VMEM((3, 256, 256), BF),
             pltpu.VMEM((2, 256, 256), BF),
             pltpu.VMEM((2, 256, 256), BF),
             pltpu.VMEM((7,) + piece, F32),
@@ -478,8 +489,8 @@
             dma((STAGES,)),
             dma((COPIES,)),
             dma((COPIES,)),
-            dma((2,)),
-            dma((2,)),
+            dma((3,)),
+            dma((3,)),
             dma((2, 2)),
             dma((2, 2)),
         ],

time: 119 us -> 118 us (level)
  no operation moved by 1% of the time
where the time goes in v4:
time: 118 us
  Pallas kernels  115 us (97%)
  other arithmetic  1.67 us (1%)
    pallas_call x1, Pallas kernels, shards(): pl.pallas_call(kernel, name='graph_layers', out_shape=jax.ShapeDtypeStruc...  115 us

profile of v4, /device:TPU:0, one launch (start us, length us, event | category | flops | bytes accessed | tf_op | source)
XLA Modules:
  0.0 117.7 jit_solution(14865480696430453954)
XLA Ops:
  0.7 115.4 %graph_layers.1 = f32[256,256]{1,0:T(8,128)} custom-call(s32[1,256]{1,0:T(1,128)} %bitcast.7, s32[1,256]{1,0:T(1,128)} %bitcast.8, s32[1,1]{1,0:T(1,128)S(6)} %copy.8.count_ref, s32[2,8]{1,0:T(2,128)} %bitcast.9, f32[2,16,8,8,256]{4,3,2,1,0:T(8,128)} %bitcast.6, f32[256,128,128]{2,1,0:T(8,128)} %bitcast.5, f32[2,256,256]{2,1,0:T(8,128)} %w_ref.1), custom_call_target="tpu_custom_call" | custom-call | tf_op jit(solution)/shard_map/graph_layers/pallas_call | solution.py:446
  116.0 1.7 %broadcast_maximum_fusion = f32[256,256]{1,0:T(8,128)} fusion(f32[256,256]{1,0:T(8,128)} %graph_layers.1), kind=kLoop, calls=%fused_computation | loop fusion | flops 65536 | bytes 524288 | tf_op jit(solution)/shard_map/max | solution.py:509

commit v5 on v4

--- a/solution.py
+++ b/solution.py
@@ -265,10 +265,12 @@
         ready((1, 1, 1), (1, 3, 1), (0, 2, 0))
         products(layer, [(1, chip(1, 1)), (1, chip(3, 1)), (0, chip(2, 0))], out, every)
         end_far(0, 1)
-        ready((1, 2, 1), (0, 2, 1))
+        ready((1, 2, 1))
+        products(layer, [(1, chip(2, 1))], out, every)
+        ready((0, 2, 1))
         for h in range(2):
             products(
-                layer, [(0, chip(2, 1)), (1, chip(2, 1))], out, rows_of[h], h == 0
+                layer, [(0, chip(2, 1))], out, rows_of[h], h == 0
             )
             begin[h]()
 

time: 118 us -> 115 us (0.975)
  Pallas kernels: 115 us -> 112 us
    pallas_call x1, Pallas kernels: 115 us -> 112 us  [shards(): pl.pallas_call(kernel, name='graph_layers', out_shape=jax.ShapeDtypeStruc...]
where the time goes in v5:
time: 115 us
  Pallas kernels  112 us (97%)
  other arithmetic  1.67 us (1%)
    pallas_call x1, Pallas kernels, shards(): pl.pallas_call(kernel, name='graph_layers', out_shape=jax.ShapeDtypeStruc...  112 us

profile of v5, /device:TPU:0, one launch (start us, length us, event | category | flops | bytes accessed | tf_op | source)
XLA Modules:
  0.0 114.8 jit_solution(11493542304777768751)
XLA Ops:
  0.7 112.5 %graph_layers.1 = f32[256,256]{1,0:T(8,128)} custom-call(s32[1,256]{1,0:T(1,128)} %bitcast.7, s32[1,256]{1,0:T(1,128)} %bitcast.8, s32[1,1]{1,0:T(1,128)S(6)} %copy.8.count_ref, s32[2,8]{1,0:T(2,128)} %bitcast.9, f32[2,16,8,8,256]{4,3,2,1,0:T(8,128)} %bitcast.6, f32[256,128,128]{2,1,0:T(8,128)} %bitcast.5, f32[2,256,256]{2,1,0:T(8,128)} %w_ref.1), custom_call_target="tpu_custom_call" | custom-call | tf_op jit(solution)/shard_map/graph_layers/pallas_call | solution.py:448
  113.1 1.7 %broadcast_maximum_fusion = f32[256,256]{1,0:T(8,128)} fusion(f32[256,256]{1,0:T(8,128)} %graph_layers.1), kind=kLoop, calls=%fused_computation | loop fusion | flops 65536 | bytes 524288 | tf_op jit(solution)/shard_map/max | solution.py:511

commit v6 on v5

--- a/solution.py
+++ b/solution.py
@@ -321,8 +321,12 @@
         def start(self):
             over = (row, reps_dev(1, 0))
             self.over = {
-                b: remote(self.part(reps_dev(1, b)), self.buf.at[b], over) for b in (2, 1, 3, 0)
+                b: remote(self.part(reps_dev(1, b)), self.buf.at[b], over) for b in (2, 1, 3)
             }
+
+        def start_last(self):
+            over = (row, reps_dev(1, 0))
+            self.over[0] = remote(self.part(reps_dev(1, 0)), self.buf.at[0], over)
 
         def near(self, b):
             self.over[b].wait_recv()
@@ -372,6 +376,7 @@
     def add_up(x_first, z_first, use):
         z_first.pass_on()
         x_first.send_far()
+        x_first.start_last()
         z_first.cross()
         x_first.send_near()
         x_first.pass_on()

time: 115 us -> 115 us (level)
  no operation moved by 1% of the time
where the time goes in v6:
time: 115 us; the launch traced here: 114 us
  Pallas kernels  112 us (97%)
  other arithmetic  1.67 us (1%)
    pallas_call x1, Pallas kernels, shards(): pl.pallas_call(kernel, name='graph_layers', out_shape=jax.ShapeDtypeStruc...  112 us

profile of v6, /device:TPU:0, one launch (start us, length us, event | category | flops | bytes accessed | tf_op | source)
XLA Modules:
  0.0 114.5 jit_solution(4661179939551307458)
XLA Ops:
  0.7 112.2 %graph_layers.1 = f32[256,256]{1,0:T(8,128)} custom-call(s32[1,256]{1,0:T(1,128)} %bitcast.7, s32[1,256]{1,0:T(1,128)} %bitcast.8, s32[1,1]{1,0:T(1,128)S(6)} %copy.8.count_ref, s32[2,8]{1,0:T(2,128)} %bitcast.9, f32[2,16,8,8,256]{4,3,2,1,0:T(8,128)} %bitcast.6, f32[256,128,128]{2,1,0:T(8,128)} %bitcast.5, f32[2,256,256]{2,1,0:T(8,128)} %w_ref.1), custom_call_target="tpu_custom_call" | custom-call | tf_op jit(solution)/shard_map/graph_layers/pallas_call | solution.py:453
  112.8 1.7 %broadcast_maximum_fusion = f32[256,256]{1,0:T(8,128)} fusion(f32[256,256]{1,0:T(8,128)} %graph_layers.1), kind=kLoop, calls=%fused_computation | loop fusion | flops 65536 | bytes 524288 | tf_op jit(solution)/shard_map/max | solution.py:516
